TPU v7x, 32 devices: a whole 2x2x4 slice. The times are simulated.
32 devices in a mesh: dp: 4 (over y, x), expert: 8 (over z, core).
Axes of the slice: x: 2, y: 2, z: 4, core: 2. Of those that a mesh axis runs over, the one named last changes fastest.
Arguments:
- tokens: bfloat16 [32768, 2048], P(('dp', 'expert')), may hold values from -16 to 16
- slot_param: bfloat16 [2048, 64], replicated, may hold values from -10 to 10
- pattern: int32 [64, 256], P(None, ('dp', 'expert')), may hold values from 0 to 1, as said below
- w_in: bfloat16 [16, 2048, 4096], P('expert', None, 'dp'), may hold values from -0.125 to 0.125
- w_out: bfloat16 [16, 4096, 2048], P('expert', 'dp'), may hold values from -0.09375 to 0.09375
Outputs:
- mixed: bfloat16 [32768, 2048], P(('dp', 'expert'))
Inputs may be any that keep to these rules, and one draw needn't show every extreme that they name: `pattern`: every slot sees at least one block; about a quarter of all pairs are 1.
All inputs are finite; a program needn't handle non-finite values.
Results may differ from a plain program's by a relative error of at most 0.0095.
Values may be sent and summed in bfloat16 or wider, within the bound.
A program may use at most 64 MiB of HBM per device.

v0:
```python
import jax
import jax.numpy as jnp
from jax import lax
from jax.sharding import PartitionSpec as P

D = 2048
EXP_DEV = 2
SLOTS = 4
BLOCK = 128


floor_value = -1e30


def local(tokens, slot_param, pattern, w_in, w_out):
    slot_count = slot_param.shape[1]
    logits = jnp.dot(tokens, slot_param, preferred_element_type=jnp.float32)
    visible = jnp.repeat(pattern.T > 0, BLOCK, axis=0)
    local_peak = jnp.max(jnp.where(visible, logits, floor_value), axis=0)
    slot_peak = lax.pmax(local_peak, ("dp", "expert"))
    weights = jnp.where(visible, jnp.exp(logits - slot_peak[None, :]), 0.0).astype(jnp.bfloat16)
    weight_sum = jnp.sum(weights.astype(jnp.float32), axis=0)
    numerator = lax.dot_general(
        weights, tokens, (((0,), (0,)), ((), ())), preferred_element_type=jnp.float32
    )
    group_count = lax.axis_size("dp")
    spread_sum = jnp.broadcast_to(weight_sum[:, None], (slot_count, group_count))
    split_num, split_den = (
        lax.psum_scatter(numerator, "dp", scatter_dimension=1, tiled=True),
        lax.psum_scatter(spread_sum, "dp", scatter_dimension=1, tiled=True),
    )
    owned_num, owned_den = (
        lax.psum_scatter(split_num, "expert", scatter_dimension=0, tiled=True),
        lax.psum_scatter(split_den, "expert", scatter_dimension=0, tiled=True),
    )
    slot_num = lax.all_gather(owned_num, "dp", axis=1, tiled=True)
    slot_den = owned_den[:, 0]
    slot_in = (slot_num / slot_den[:, None]).astype(jnp.bfloat16)
    grouped = slot_in.reshape(EXP_DEV, SLOTS, D)
    hidden = jax.nn.gelu(
        jnp.einsum("esd,edh->esh", grouped, w_in, preferred_element_type=jnp.float32)
    ).astype(jnp.bfloat16)
    partial_value = jnp.einsum(
        "esh,ehd->esd", hidden, w_out, preferred_element_type=jnp.float32
    ).reshape(EXP_DEV * SLOTS, D)
    mixing = jax.nn.softmax(logits, axis=1).astype(jnp.bfloat16)
    owned_out = lax.psum(partial_value, "dp").astype(jnp.bfloat16)
    slot_out = lax.all_gather(owned_out, "expert", axis=0, tiled=True)
    result = jnp.dot(mixing, slot_out, preferred_element_type=jnp.float32)
    return result.astype(jnp.bfloat16)


def solution(mesh):
    return jax.shard_map(
        local,
        mesh=mesh,
        in_specs=(
            P(("dp", "expert"), None),
            P(),
            P(None, ("dp", "expert")),
            P("expert", None, "dp"),
            P("expert", "dp", None),
        ),
        out_specs=P(("dp", "expert"), None),
        check_vma=False,
    )
```

profile of v0, /device:TPU:0, one launch (start us, length us, event | category | flops | bytes accessed | tf_op | source)
XLA Modules:
  0.0 171.8 jit_solution(6145641477331126118)
XLA Ops:
  6.5 0.0 copy-start
  6.5 0.0 copy-start.2
  6.5 0.0 copy-start.1
  6.5 0.0 reduce-scatter.4.cloned.1.call-start
  6.5 0.7 compare_bitcast_fusion
  7.3 0.1 copy.7
  7.4 0.1 copy-done
  7.5 3.6 %fusion.22 = (f32[1024]{0:T(1024)S(1)}, f32[1024,64]{0,1:T(8,128)S(1)}) fusion(bf16[1024,2048]{1,0:T(8,128)(2,1)} %param.5, bf16[2048,64]{0,1:T(8,128)(2,1)S(1)} %copy-done), kind=kOutput, calls=%fused_computation.32 | convolution fusion | flops 268499968 | bytes 4722688 | tf_op jit(solution)/shard_map/dot_general | solution.py:17
  11.1 0.1 broadcast_in_dim.19
  11.2 0.2 fusion
  11.4 42.0 %pmax.7 = f32[64]{0:T(128)S(1)} all-reduce(f32[64]{0:T(128)S(1)} %get-tuple-element.6), channel_id=1, replica_groups=mesh['dp'=4,'expert'=8] {'dp','expert'}, use_global_device_ids=true, to_apply=%region_3.4 | all-reduce | flops 64 | bytes 512 | tf_op jit(solution)/shard_map/pmax | solution.py:20
  53.4 0.2 convert_reduce_fusion
  53.6 3.8 %fusion.25 = f32[64,2048]{1,0:T(8,128)} fusion(bf16[1024,64]{0,1:T(8,128)(2,1)S(1)} %get-tuple-element.8, bf16[1024,2048]{1,0:T(8,128)(2,1)} %param.5), kind=kOutput, calls=%fused_computation.34 | convolution fusion | flops 268435456 | bytes 4849664 | tf_op jit(solution)/shard_map/dot_general | solution.py:23
  57.5 0.0 reduce-scatter.4.cloned.1.call-update
  57.5 0.0 reduce-scatter.6.cloned.1.call-start
  57.6 24.7 %reduce-scatter.4.cloned.1.call-done = f32[64,512]{1,0:T(8,128)} async-done(((f32[64,2048]{1,0:T(8,128)}), f32[64,512]{1,0:T(8,128)}) %reduce-scatter.4.cloned.1.call-update) | async-done | bytes 131088 | tf_op jit(solution)/shard_map/reduce_scatter | solution.py:29
  82.3 0.0 reduce-scatter.6.cloned.1.call-update
  82.3 0.0 copy-done.2
  82.3 0.7 dynamic-slice.2
  83.0 0.0 copy-done.1
  83.0 0.6 dynamic-slice
  84.3 8.9 %all-reduce = f32[64,4]{0,1:T(4,128)S(1)} all-reduce(f32[64,4]{0,1:T(4,128)S(1)} %broadcast_in_dim.22), channel_id=4, replica_groups=mesh['dp'=4,'expert'=8] {'dp'}, use_global_device_ids=true, to_apply=%region_7.8.clone | all-reduce | flops 256 | bytes 2048
  93.2 0.6 constant_dynamic-slice_fusion.1
  93.8 14.2 %all-reduce.1 = f32[64,1]{0,1:T(1,128)S(1)} all-reduce(f32[64,1]{0,1:T(1,128)S(1)} %constant_dynamic-slice_fusion.1), channel_id=5, replica_groups=mesh['dp'=4,'expert'=8] {'expert'}, use_global_device_ids=true, to_apply=%region_8.9.clone | all-reduce | flops 64 | bytes 512
  108.1 0.1 fusion.17
  108.2 6.6 %reduce-scatter.6.cloned.1.call-done = f32[8,512]{1,0:T(8,128)} async-done(((f32[64,512]{1,0:T(8,128)}), f32[8,512]{1,0:T(8,128)}) %reduce-scatter.6.cloned.1.call-update) | async-done | bytes 16400 | tf_op jit(solution)/shard_map/reduce_scatter | solution.py:33
  114.8 8.4 %all_gather.6 = f32[8,2048]{1,0:T(8,128)S(1)} all-gather(f32[8,512]{1,0:T(8,128)} %reduce-scatter.6.cloned.1.call-done), channel_id=1, replica_groups=mesh['dp'=4,'expert'=8] {'dp'}, dimensions={1}, use_global_device_ids=true | all-gather | bytes 81920 | tf_op jit(solution)/shard_map/all_gather | solution.py:36
  123.2 0.1 divide_convert_fusion.2
  123.3 8.0 %fusion.11 = f32[2,4,2048]{2,1,0:T(4,128)S(1)} fusion(bf16[2,1024,2048]{2,1,0:T(8,128)(2,1)} %param.9, bf16[2,4,2048]{2,1,0:T(4,128)(2,1)S(1)} %reshape.14, bf16[2,2048,1024]{2,1,0:T(8,128)(2,1)} %param.8), kind=kOutput, calls=%fused_computation.19 | convolution fusion | flops 67182592 | bytes 16875520 | tf_op jit(solution)/shard_map/esh,ehd->esd/dot_general | solution.py:43
  131.4 16.1 %psum.7 = bf16[8,2048]{1,0:T(8,128)(2,1)S(1)} all-reduce(f32[8,2048]{1,0:T(8,128)S(1)} %reshape.15), channel_id=1, replica_groups=mesh['dp'=4,'expert'=8] {'dp'}, use_global_device_ids=true, to_apply=%region_9.10 | all-reduce | flops 16384 | bytes 98304 | tf_op jit(solution)/shard_map/psum | solution.py:47
  147.4 14.2 %all_gather.7 = bf16[64,2048]{1,0:T(8,128)(2,1)S(1)} all-gather(bf16[8,2048]{1,0:T(8,128)(2,1)S(1)} %psum.7), channel_id=1, replica_groups=mesh['dp'=4,'expert'=8] {'expert'}, dimensions={0}, use_global_device_ids=true | all-gather | bytes 294912 | tf_op jit(solution)/shard_map/all_gather | solution.py:48
  161.6 3.3 %convolution_convert_fusion = bf16[1024,2048]{1,0:T(8,128)(2,1)} fusion(bf16[64,2048]{1,0:T(8,128)(2,1)S(1)} %all_gather.7, f32[1024,64]{0,1:T(8,128)S(1)} %get-tuple-element.10, f32[1024]{0:T(1024)S(1)} %get-tuple-element.5, f32[1024]{0:T(1024)S(1)} %get-tuple-element.9), kind=kOutput, calls=%fused_computation | convolution fusion | flops 270729216 | bytes 4726784 | tf_op jit(solution)/shard_map/dot_general | solution.py:49
  (3 shorter events, 0.1 us)
Async XLA Ops:
  6.5 1.0 copy-start
  6.5 75.8 %copy-start.2 = (u32[32]{0:T(128)S(1)}, u32[32]{0:T(128)}, u32[]{:S(2)}) copy-start(u32[32]{0:T(128)} %constant.26) | copy-start | bytes 388
  6.5 76.4 %copy-start.1 = (u32[32]{0:T(128)S(1)}, u32[32]{0:T(128)}, u32[]{:S(2)}) copy-start(u32[32]{0:T(128)} %constant.22) | copy-start | bytes 388
  6.5 75.7 %reduce-scatter.4.cloned.1.call-start = ((), (), s32[]{:S(2)}) async-start(), calls=%async_computation.2 | async-start | bytes 655360 | tf_op jit(solution)/shard_map/reduce_scatter | solution.py:29
  57.5 57.3 %reduce-scatter.6.cloned.1.call-start = ((), (), s32[]{:S(2)}) async-start(), calls=%async_computation.3 | async-start | bytes 147456 | tf_op jit(solution)/shard_map/reduce_scatter | solution.py:33
Sparse Core Ops, SparseCore 0:
  57.6 24.6 reduce-scatter.3
  84.6 30.1 reduce-scatter.5
where the time goes:
time: 172 us
  blocking collectives  104 us (60%)
  waiting for transfers between devices  31.4 us (18%)
  matrix products  18.8 us (11%)
  between operations  14.2 us (8%)
  local copies, waits for them, and re-layouts  2.38 us (1%)
    pmax x1, blocking collectives, local(): slot_peak = lax.pmax(local_peak, ('dp', 'expert'))  42 us
    reduce_scatter x1, waiting for transfers between devices, local(): lax.psum_scatter(numerator, 'dp', scatter_dimension=1, tiled=True)  24.7 us
    unnamed x2, blocking collectives  23.2 us
    psum x1, blocking collectives, local(): owned_out = lax.psum(partial_value, 'dp').astype(jnp.bfloat16)  16.1 us
    all_gather x1, blocking collectives, local(): slot_out = lax.all_gather(owned_out, 'expert', axis=0, tiled=True)  14.2 us
    all_gather x1, blocking collectives, local(): slot_num = lax.all_gather(owned_num, 'dp', axis=1, tiled=True)  8.38 us
    dot_general x1, matrix products, local(): jnp.einsum('esh,ehd->esd', hidden, w_out, preferred_element_type=jnp.floa...  8.04 us
    reduce_scatter x1, waiting for transfers between devices, local(): lax.psum_scatter(split_num, 'expert', scatter_dimension=0, tiled=True)  6.64 us
  transfers between devices with their start and end apart: 2, of which 2 were waited for; matrix products, arithmetic and copies ran while one was open for 1% of the time, Pallas kernels for 0%

commit v1 on v0

v1 whole, which is shorter than its diff:
```python
import functools

import jax
import jax.numpy as jnp
from jax import lax
from jax.experimental import pallas as pl
from jax.experimental.pallas import tpu as pltpu
from jax.sharding import PartitionSpec as P

MESH = pl.DeviceIdType.MESH
floor_value = -1e30
F32, BF16 = jnp.float32, jnp.bfloat16


def nt_dot(a, b):
    return lax.dot_general(a, b, (((1,), (1,)), ((), ())), preferred_element_type=F32)


def gelu(x):
    return 0.5 * x * (1.0 + jnp.tanh(0.7978845608028654 * (x + 0.044715 * (x * x * x))))


def fold(x):
    half = x.shape[1] // 2
    return jnp.concatenate([x[:, :half], x[:, half:]], axis=0).astype(BF16)


def unfold(x):
    rows = x.shape[0] // 2
    wide = x.astype(F32)
    return jnp.concatenate([wide[:rows], wide[rows:]], axis=1)


def slots_kernel(
    n_dp, n_ex, pieces,
    tok_hbm, slot_ref, pat_ref, win_hbm, wout_hbm,
    mix_ref, out_ref,
    tok, win, wout, logits, wts,
    stat1, num1, rstat1, rnum1,
    send2, recv2, xs, rx, part, rpart, own5, recv5, full6, recv6,
    tok_sem, w_sem,
    ss1, rs1, sn1, rn1, s2, r2, s3, r3, s4, r4, s5, r5, s6, r6,
):
    d, k = lax.axis_index("dp"), lax.axis_index("expert")
    slots, width = slot_ref.shape
    rows = tok.shape[0]
    cols = width // n_dp
    per_dev = slots // n_ex
    exp_dev, _, hid = win.shape
    blocks = pat_ref.shape[0]
    block = rows // blocks
    lanes = stat1.shape[1]
    piece = rows // pieces
    folded = recv5.dtype == BF16

    def to_dp(src, dst, ssem, rsem, i):
        return pltpu.make_async_remote_copy(
            src_ref=src, dst_ref=dst, send_sem=ssem.at[i], recv_sem=rsem.at[i],
            device_id={"dp": lax.rem(d + i, n_dp)}, device_id_type=MESH,
        )

    def to_ex(src, dst, ssem, rsem, i):
        return pltpu.make_async_remote_copy(
            src_ref=src, dst_ref=dst, send_sem=ssem.at[i], recv_sem=rsem.at[i],
            device_id={"expert": lax.rem(k + i, n_ex)}, device_id_type=MESH,
        )

    loads = [
        pltpu.make_async_copy(
            tok_hbm.at[pl.ds(c * piece, piece)], tok.at[pl.ds(c * piece, piece)], tok_sem.at[c]
        )
        for c in range(pieces)
    ]
    for load in loads:
        load.start()
    barrier = pltpu.get_barrier_semaphore()
    for i in range(1, n_dp):
        pl.semaphore_signal(
            barrier, inc=1, device_id={"dp": lax.rem(d + i, n_dp)}, device_id_type=MESH
        )
    for i in range(1, n_ex):
        pl.semaphore_signal(
            barrier, inc=1, device_id={"expert": lax.rem(k + i, n_ex)}, device_id_type=MESH
        )
    load_in = pltpu.make_async_copy(win_hbm, win, w_sem.at[0])
    load_out = pltpu.make_async_copy(wout_hbm, wout, w_sem.at[1])

    row_id = lax.broadcasted_iota(jnp.int32, (slots, lanes), 0)
    lane_id = lax.broadcasted_iota(jnp.int32, (slots, lanes), 1)
    eye = row_id == lane_id

    def as_column(row):
        return jnp.sum(jnp.where(eye, row, 0.0), axis=1, keepdims=True)

    def as_row(column):
        return jnp.sum(jnp.where(eye, column, 0.0), axis=0, keepdims=True)

    slot_t = slot_ref[...]
    for c in range(pieces):
        loads[c].wait()
        if c == pieces - 1:
            load_in.start()
            load_out.start()
        logits[:, c * piece:(c + 1) * piece] = nt_dot(slot_t, tok[c * piece:(c + 1) * piece, :])

    seen = pat_ref[...].astype(F32)
    if lanes > slots:
        seen = jnp.concatenate([seen, jnp.zeros((blocks, lanes - slots), F32)], axis=1)
    columns = [as_column(seen[b:b + 1, :]) > 0.0 for b in range(blocks)]
    masked = [
        jnp.where(columns[b], logits[:, b * block:(b + 1) * block], floor_value)
        for b in range(blocks)
    ]
    top = masked[0]
    for b in range(1, blocks):
        top = jnp.maximum(top, masked[b])
    peak = jnp.max(top, axis=1, keepdims=True)
    total = jnp.zeros((slots, block), F32)
    for b in range(blocks):
        shifted = jnp.where(columns[b], masked[b] - peak, floor_value)
        weight = jnp.exp(shifted).astype(BF16)
        wts[:, b * block:(b + 1) * block] = weight
        total = total + weight.astype(F32)
    den = jnp.sum(total, axis=1, keepdims=True)
    stat_row = lax.broadcasted_iota(jnp.int32, stat1.shape, 0)
    stat1[...] = jnp.where(stat_row == 0, as_row(peak), as_row(den))

    pl.semaphore_wait(barrier, n_dp - 1 + n_ex - 1)
    stat_copies = [to_dp(stat1, rstat1.at[i], ss1, rs1, i) for i in range(1, n_dp)]
    for copy in stat_copies:
        copy.start()
    weights = wts[...]
    num_copies = []
    for i in list(range(1, n_dp)) + [0]:
        target = lax.rem(d + i, n_dp)
        strip = tok[:, pl.ds(pl.multiple_of(target * cols, cols), cols)]
        num1[i] = jnp.dot(weights, strip, preferred_element_type=F32).astype(BF16)
        if i:
            copy = to_dp(num1.at[i], rnum1.at[i], sn1, rn1, i)
            copy.start()
            num_copies.append(copy)

    raw = logits[...]
    risen = jnp.exp(raw - jnp.max(raw, axis=0, keepdims=True))
    mix_ref[...] = (risen / jnp.sum(risen, axis=0, keepdims=True)).astype(BF16)

    for copy in stat_copies:
        copy.wait_recv()
    stats = [stat1[...]] + [rstat1[i] for i in range(1, n_dp)]
    group_peak = stats[0][0:1]
    for stat in stats[1:]:
        group_peak = jnp.maximum(group_peak, stat[0:1])
    scales = [jnp.exp(stat[0:1] - group_peak) for stat in stats]
    group_den = stats[0][1:2] * scales[0]
    for stat, scale in zip(stats[1:], scales[1:]):
        group_den = group_den + stat[1:2] * scale
    scales = [as_column(scale) for scale in scales]
    tail = jnp.where(lane_id == 0, as_column(group_peak), as_column(group_den))
    send2[:, :, cols:] = tail.reshape(n_ex, per_dev, lanes)
    group_num = scales[0] * num1[0].astype(F32)
    for i in range(1, n_dp):
        num_copies[i - 1].wait_recv()
        group_num = group_num + scales[i] * rnum1[i].astype(F32)
    send2[:, :, :cols] = group_num.reshape(n_ex, per_dev, cols)

    copies2 = []
    for i in range(1, n_ex):
        copy = to_ex(send2.at[lax.rem(k + i, n_ex)], recv2.at[i], s2, r2, i)
        copy.start()
        copies2.append(copy)
    for copy in copies2:
        copy.wait_recv()
    given = [send2[k]] + [recv2[i] for i in range(1, n_ex)]
    last_peak = given[0][:, cols:cols + 1]
    for item in given[1:]:
        last_peak = jnp.maximum(last_peak, item[:, cols:cols + 1])
    num = jnp.zeros((per_dev, cols), F32)
    den = jnp.zeros((per_dev, 1), F32)
    for item in given:
        scale = jnp.exp(item[:, cols:cols + 1] - last_peak)
        num = num + scale * item[:, :cols]
        den = den + scale * item[:, cols + 1:cols + 2]
    xs[...] = (num / den).astype(BF16).astype(F32)

    copies3 = [to_dp(xs, rx.at[i], s3, r3, i) for i in range(1, n_dp)]
    for copy in copies3:
        copy.start()
    load_in.wait()
    sums = [jnp.zeros((per_dev, hid), F32) for _ in range(exp_dev)]
    for i in range(n_dp):
        if i:
            copies3[i - 1].wait_recv()
        x = (rx[i] if i else xs[...]).astype(BF16)
        start = pl.multiple_of(lax.rem(d + n_dp - i, n_dp) * cols, cols)
        for e in range(exp_dev):
            sums[e] = sums[e] + jnp.dot(
                x, win[e, pl.ds(start, cols), :], preferred_element_type=F32
            )
    hidden = [gelu(s).astype(BF16) for s in sums]
    load_out.wait()
    own_slots = per_dev // exp_dev
    owner = lax.broadcasted_iota(jnp.int32, (per_dev, cols), 0) // own_slots
    copies4 = []
    for i in list(range(1, n_dp)) + [0]:
        start = pl.multiple_of(lax.rem(d + i, n_dp) * cols, cols)
        value = jnp.zeros((per_dev, cols), F32)
        for e in range(exp_dev):
            made = jnp.dot(hidden[e], wout[e, :, pl.ds(start, cols)], preferred_element_type=F32)
            value = jnp.where(owner == e, made, value)
        part[i] = value
        if i:
            copy = to_dp(part.at[i], rpart.at[i], s4, r4, i)
            copy.start()
            copies4.append(copy)
    value = part[0]
    for i in range(1, n_dp):
        copies4[i - 1].wait_recv()
        value = value + rpart[i]

    own5[...] = fold(value) if folded else value.astype(BF16).astype(F32)
    copies5 = [to_ex(own5, recv5.at[i], s5, r5, i) for i in range(1, n_ex)]
    for copy in copies5:
        copy.start()
    for copy in copies2:
        copy.wait_send()
    for i in range(n_ex):
        if i:
            copies5[i - 1].wait_recv()
        item = recv5[i] if i else own5[...]
        source = lax.rem(k + n_ex - i, n_ex)
        send2[source, :, :cols] = unfold(item) if folded else item
    full6[...] = send2[:, :, :cols].reshape(slots, cols).astype(BF16)
    copies6 = [to_dp(full6, recv6.at[i], s6, r6, i) for i in range(1, n_dp)]
    for copy in copies6:
        copy.start()
    for i in range(n_dp):
        if i:
            copies6[i - 1].wait_recv()
        start = pl.multiple_of(lax.rem(d + n_dp - i, n_dp) * cols, cols)
        out_ref[:, pl.ds(start, cols)] = recv6[i] if i else full6[...]
    for copy in stat_copies + num_copies + copies3 + copies4 + copies5 + copies6:
        copy.wait_send()


def local(n_dp, n_ex, tokens, slot_param, pattern, w_in, w_out):
    rows, width = tokens.shape
    slots = slot_param.shape[1]
    cols = width // n_dp
    per_dev = slots // n_ex
    lanes = -(-slots // 128) * 128
    pieces = 4
    item = ((2 * per_dev, cols // 2), BF16) if cols % 256 == 0 else ((per_dev, cols), F32)
    dma = pltpu.SemaphoreType.DMA
    vmem, anywhere = pl.BlockSpec(memory_space=pltpu.VMEM), pl.BlockSpec(memory_space=pl.ANY)
    mixing, slot_out = pl.pallas_call(
        functools.partial(slots_kernel, n_dp, n_ex, pieces),
        out_shape=(
            jax.ShapeDtypeStruct((slots, rows), BF16),
            jax.ShapeDtypeStruct((slots, width), BF16),
        ),
        in_specs=[anywhere, vmem, vmem, anywhere, anywhere],
        out_specs=(vmem, vmem),
        scratch_shapes=[
            pltpu.VMEM((rows, width), BF16),
            pltpu.VMEM(w_in.shape, BF16),
            pltpu.VMEM(w_out.shape, BF16),
            pltpu.VMEM((slots, rows), F32),
            pltpu.VMEM((slots, rows), BF16),
            pltpu.VMEM((8, lanes), F32),
            pltpu.VMEM((n_dp, slots, cols), BF16),
            pltpu.VMEM((n_dp, 8, lanes), F32),
            pltpu.VMEM((n_dp, slots, cols), BF16),
            pltpu.VMEM((n_ex, per_dev, cols + lanes), F32),
            pltpu.VMEM((n_ex, per_dev, cols + lanes), F32),
            pltpu.VMEM((per_dev, cols), F32),
            pltpu.VMEM((n_dp, per_dev, cols), F32),
            pltpu.VMEM((n_dp, per_dev, cols), F32),
            pltpu.VMEM((n_dp, per_dev, cols), F32),
            pltpu.VMEM(*item),
            pltpu.VMEM((n_ex,) + item[0], item[1]),
            pltpu.VMEM((slots, cols), BF16),
            pltpu.VMEM((n_dp, slots, cols), BF16),
            dma((pieces,)),
            dma((2,)),
        ]
        + [dma((n,)) for n in (n_dp, n_dp, n_ex, n_dp, n_dp, n_ex, n_dp) for _ in range(2)],
        compiler_params=pltpu.CompilerParams(
            collective_id=0, has_side_effects=True, vmem_limit_bytes=60 * 1024 * 1024
        ),
        cost_estimate=pl.CostEstimate(
            flops=4 * rows * width * slots + 4 * per_dev * w_in.size // w_in.shape[0],
            bytes_accessed=2 * (tokens.size + w_in.size + w_out.size),
            transcendentals=2 * rows * slots,
        ),
    )(tokens, slot_param.T, pattern.T, w_in, w_out)
    result = lax.dot_general(
        mixing, slot_out, (((0,), (0,)), ((), ())), preferred_element_type=F32
    )
    return result.astype(BF16)


def solution(mesh):
    return jax.shard_map(
        functools.partial(local, mesh.shape["dp"], mesh.shape["expert"]),
        mesh=mesh,
        in_specs=(
            P(("dp", "expert"), None),
            P(),
            P(None, ("dp", "expert")),
            P("expert", None, "dp"),
            P("expert", "dp", None),
        ),
        out_specs=P(("dp", "expert"), None),
        check_vma=False,
    )
```

time: 172 us -> 41 us (0.24)
  blocking collectives: 104 us -> 0 us
  Pallas kernels: 0 us -> 36.6 us
  waiting for transfers between devices: 31.4 us -> 0 us
  matrix products: 18.8 us -> 4.31 us
  between operations: 14.2 us -> 0.01 us
  local copies, waits for them, and re-layouts: 2.38 us -> 0 us
    pmax x1 -> x0, blocking collectives: 42 us -> none  [local(): slot_peak = lax.pmax(local_peak, ('dp', 'expert'))]
    pallas_call x0 -> x1, Pallas kernels: none -> 36.6 us  [local(): pl.pallas_call(functools.partial(slots_kernel, n_dp, n_ex, pieces), out_s...]
    reduce_scatter x2 -> x0, waiting for transfers between devices: 31.4 us -> none  [the longest x1 24.7 us: local(): lax.psum_scatter(numerator, 'dp', scatter_dimension=1, tiled=True)]
    unnamed x2 -> x0, blocking collectives: 23.2 us -> none
    all_gather x2 -> x0, blocking collectives: 22.6 us -> none  [the longest x1 14.2 us: local(): slot_out = lax.all_gather(owned_out, 'expert', axis=0, tiled=True)]
    psum x1 -> x0, blocking collectives: 16.1 us -> none  [local(): owned_out = lax.psum(partial_value, 'dp').astype(jnp.bfloat16)]
    dot_general x4 -> x1, matrix products: 18.8 us -> 4.31 us  [local(): lax.dot_general(mixing, slot_out, (((0,), (0,)), ((), ())), preferred_ele...]
    unnamed x9 -> x0, local copies, waits for them, and re-layouts: 2.01 us -> none
  transfers between devices with their start and end apart: 2 -> 0, of which waited for: 2 -> 0; matrix products, arithmetic and copies ran while one was open for 1% -> 0% of each run, Pallas kernels for 0% -> 0%
where the time goes in v1:
time: 41 us; the launch traced here: 40.9 us
  Pallas kernels  36.6 us (89%)
  matrix products  4.31 us (11%)
    pallas_call x1, Pallas kernels, local(): pl.pallas_call(functools.partial(slots_kernel, n_dp, n_ex, pieces), out_s...  36.6 us
    dot_general x1, matrix products, local(): lax.dot_general(mixing, slot_out, (((0,), (0,)), ((), ())), preferred_ele...  4.31 us

profile of v1, /device:TPU:0, one launch (start us, length us, event | category | flops | bytes accessed | tf_op | source)
XLA Modules:
  0.0 40.9 jit_solution(2420858141953597917)
XLA Ops:
  0.0 36.6 %shard_map.55 = (bf16[64,1024]{1,0:T(8,128)(2,1)}, bf16[64,2048]{1,0:T(8,128)(2,1)}) custom-call(bf16[1024,2048]{1,0:T(8,128)(2,1)} %tok_hbm.1, bf16[64,2048]{1,0:T(8,128)(2,1)} %bitcast.4, s32[8,64]{1,0:T(8,128)} %bitcast.5, bf16[2,2048,1024]{2,1,0:T(8,128)(2,1)} %win_hbm.1, bf16[2,1024,2048]{2,1,0:T(8,128)(2,1)} %wout_hbm.1), custom_call_target="tpu_custom_call" | custom-call | flops 603979776 | bytes 20971520 | tf_op jit(solution)/shard_map/pallas_call | solution.py:255
  36.6 4.3 %convolution_convert_fusion = bf16[1024,2048]{1,0:T(8,128)(2,1)} fusion(bf16[64,1024]{1,0:T(8,128)(2,1)} %get-tuple-element.7, bf16[64,2048]{1,0:T(8,128)(2,1)} %get-tuple-element.8), kind=kOutput, calls=%fused_computation | convolution fusion | flops 270532608 | bytes 4587520 | tf_op jit(solution)/shard_map/dot_general | solution.py:296

commit v2 on v1

v2 whole, which is shorter than its diff:
```python
import functools

import jax
import jax.numpy as jnp
from jax import lax
from jax.experimental import pallas as pl
from jax.experimental.pallas import tpu as pltpu
from jax.sharding import PartitionSpec as P

MESH = pl.DeviceIdType.MESH
floor_value = -1e30
F32, BF16 = jnp.float32, jnp.bfloat16


def nt_dot(a, b):
    return lax.dot_general(a, b, (((1,), (1,)), ((), ())), preferred_element_type=F32)


def gelu(x):
    return 0.5 * x * (1.0 + jnp.tanh(0.7978845608028654 * (x + 0.044715 * (x * x * x))))


def fold(x):
    half = x.shape[1] // 2
    return jnp.concatenate([x[:, :half], x[:, half:]], axis=0).astype(BF16)


def flip(me, i, n):
    if n & (n - 1):
        return lax.rem(me + i, n), lax.rem(me + n - i, n)
    other, bit = 0, 1
    while bit < n:
        own = lax.rem(me // bit, 2)
        other = other + bit * ((1 - own) if i & bit else own)
        bit *= 2
    return other, other


def unfold(x):
    rows = x.shape[0] // 2
    wide = x.astype(F32)
    return jnp.concatenate([wide[:rows], wide[rows:]], axis=1)


def slots_kernel(
    n_dp, n_ex, pieces,
    tok_hbm, slot_hbm, pat_hbm, win_hbm, wout_hbm,
    out_ref,
    slot_ref, pat_ref, tok, win, wout, logits, wts, mix,
    stat1, rstat1, num1, rnum1, stat2, rstat2,
    send2, recv2, xs, rx, part, rpart, own5, recv5, recv6,
    tok_sem, w_sem,
    ss1, rs1, sn1, rn1, ss2, rs2, s2, r2, s3, r3, s4, r4, s5, r5, s6, r6,
):
    d, k = lax.axis_index("dp"), lax.axis_index("expert")
    slots, width = slot_ref.shape
    rows = tok.shape[0]
    cols = width // n_dp
    per_dev = slots // n_ex
    exp_dev, _, hid = win.shape
    blocks = pat_ref.shape[0]
    block = rows // blocks
    lanes = stat1.shape[1]
    piece = rows // pieces
    folded = recv5.dtype == BF16

    dp_to, dp_from = zip(*[flip(d, i, n_dp) for i in range(n_dp)])
    ex_to, ex_from = zip(*[flip(k, i, n_ex) for i in range(n_ex)])

    def to_dp(src, dst, ssem, rsem, i):
        return pltpu.make_async_remote_copy(
            src_ref=src, dst_ref=dst, send_sem=ssem, recv_sem=rsem,
            device_id={"dp": dp_to[i]}, device_id_type=MESH,
        )

    def to_ex(src, dst, ssem, rsem, i):
        return pltpu.make_async_remote_copy(
            src_ref=src, dst_ref=dst, send_sem=ssem, recv_sem=rsem,
            device_id={"expert": ex_to[i]}, device_id_type=MESH,
        )

    def strip(index):
        return pl.ds(pl.multiple_of(index * cols, cols), cols)

    def launch(copies):
        for copy in copies:
            copy.start()
        return copies

    loads = [
        pltpu.make_async_copy(
            tok_hbm.at[pl.ds(c * piece, piece)], tok.at[pl.ds(c * piece, piece)], tok_sem.at[c]
        )
        for c in range(pieces)
    ]
    load_slot = pltpu.make_async_copy(slot_hbm, slot_ref, w_sem.at[2])
    load_pat = pltpu.make_async_copy(pat_hbm, pat_ref, w_sem.at[3])
    for load in [load_slot, load_pat] + loads:
        load.start()
    barrier = pltpu.get_barrier_semaphore()
    for i in range(1, n_dp):
        pl.semaphore_signal(
            barrier, inc=1, device_id={"dp": dp_to[i]}, device_id_type=MESH
        )
    for i in range(1, n_ex):
        pl.semaphore_signal(
            barrier, inc=1, device_id={"expert": ex_to[i]}, device_id_type=MESH
        )
    load_in = pltpu.make_async_copy(win_hbm, win, w_sem.at[0])
    load_out = pltpu.make_async_copy(wout_hbm, wout, w_sem.at[1])

    row_id = lax.broadcasted_iota(jnp.int32, (slots, lanes), 0)
    lane_id = lax.broadcasted_iota(jnp.int32, (slots, lanes), 1)
    eye = row_id == lane_id

    def as_column(row):
        return jnp.sum(jnp.where(eye, row, 0.0), axis=1, keepdims=True)

    def as_row(column):
        return jnp.sum(jnp.where(eye, column, 0.0), axis=0, keepdims=True)

    load_slot.wait()
    load_pat.wait()
    slot_t = slot_ref[...]
    for c in range(pieces):
        loads[c].wait()
        if c == pieces - 1:
            load_in.start()
            load_out.start()
        logits[:, c * piece:(c + 1) * piece] = nt_dot(slot_t, tok[c * piece:(c + 1) * piece, :])

    seen = pat_ref[...].astype(F32)
    if lanes > slots:
        seen = jnp.concatenate([seen, jnp.zeros((blocks, lanes - slots), F32)], axis=1)
    columns = [as_column(seen[b:b + 1, :]) > 0.0 for b in range(blocks)]
    masked = [
        jnp.where(columns[b], logits[:, b * block:(b + 1) * block], floor_value)
        for b in range(blocks)
    ]
    top = masked[0]
    for b in range(1, blocks):
        top = jnp.maximum(top, masked[b])
    peak = jnp.max(top, axis=1, keepdims=True)
    total = jnp.zeros((slots, block), F32)
    for b in range(blocks):
        shifted = jnp.where(columns[b], masked[b] - peak, floor_value)
        weight = jnp.exp(shifted).astype(BF16)
        wts[:, b * block:(b + 1) * block] = weight
        total = total + weight.astype(F32)
    den = jnp.sum(total, axis=1, keepdims=True)
    stat_row = lax.broadcasted_iota(jnp.int32, stat1.shape, 0)
    stat1[...] = jnp.where(stat_row == 0, as_row(peak), as_row(den))

    pl.semaphore_wait(barrier, n_dp - 1 + n_ex - 1)
    dp_far = list(range(n_dp - 1, 0, -1))
    ex_far = list(range(n_ex - 1, 0, -1))
    stat_copies = launch(
        [to_dp(stat1, rstat1.at[i], ss1.at[i], rs1.at[i], i) for i in dp_far]
    )
    weights = wts[...]
    num_copies = {}
    for i in dp_far + [0]:
        num1[i] = jnp.dot(
            weights, tok[:, strip(dp_to[i])], preferred_element_type=F32
        ).astype(BF16)
        if i:
            num_copies[i] = to_dp(num1.at[i], rnum1.at[i], sn1.at[i], rn1.at[i], i)
            num_copies[i].start()

    for copy in stat_copies:
        copy.wait_recv()

    def join(stats):
        high = stats[0][0:1]
        for stat in stats[1:]:
            high = jnp.maximum(high, stat[0:1])
        low = stats[0][1:2] * jnp.exp(stats[0][0:1] - high)
        for stat in stats[1:]:
            low = low + stat[1:2] * jnp.exp(stat[0:1] - high)
        return high, low

    stats = [stat1[...]] + [rstat1[i] for i in range(1, n_dp)]
    high, low = join(stats)
    stat2[...] = jnp.where(stat_row == 0, high, low)
    stat2_copies = launch(
        [to_ex(stat2, rstat2.at[i], ss2.at[i], rs2.at[i], i) for i in ex_far]
    )

    raw = logits[...]
    risen = jnp.exp(raw - jnp.max(raw, axis=0, keepdims=True))
    mix[...] = (risen / jnp.sum(risen, axis=0, keepdims=True)).T.astype(BF16)

    for copy in stat2_copies:
        copy.wait_recv()
    high, low = join([stat2[...]] + [rstat2[i] for i in range(1, n_ex)])
    scales = [as_column(jnp.exp(stat[0:1] - high) / low) for stat in stats]
    joint = scales[0] * num1[0].astype(F32)
    for i in range(1, n_dp):
        num_copies[i].wait_recv()
        joint = joint + scales[i] * rnum1[i].astype(F32)
    joint = joint.reshape(n_ex, per_dev, cols)
    if folded:
        joint = jnp.concatenate([joint[:, :, :cols // 2], joint[:, :, cols // 2:]], axis=1)
    send2[...] = joint.astype(send2.dtype)

    copies2 = launch(
        [to_ex(send2.at[ex_to[i]], recv2.at[i], s2.at[i], r2.at[i], i) for i in ex_far]
    )
    value = send2[k].astype(F32)
    for copy in copies2:
        copy.wait_recv()
    for i in range(1, n_ex):
        value = value + recv2[i].astype(F32)
    xs[...] = value.astype(BF16).astype(xs.dtype)

    copies3 = launch([to_dp(xs, rx.at[i], s3.at[i], r3.at[i], i) for i in range(1, n_dp)])
    load_in.wait()
    sums = [jnp.zeros((per_dev, hid), F32) for _ in range(exp_dev)]
    for i in range(n_dp):
        if i:
            copies3[i - 1].wait_recv()
        x = rx[i] if i else xs[...]
        x = (unfold(x) if folded else x).astype(BF16)
        start = pl.multiple_of(dp_from[i] * cols, cols)
        for e in range(exp_dev):
            sums[e] = sums[e] + jnp.dot(
                x, win[e, pl.ds(start, cols), :], preferred_element_type=F32
            )
    hidden = [gelu(s).astype(BF16) for s in sums]
    load_out.wait()
    own_slots = per_dev // exp_dev
    owner = lax.broadcasted_iota(jnp.int32, (per_dev, cols), 0) // own_slots
    copies4 = {}
    for i in dp_far + [0]:
        value = jnp.zeros((per_dev, cols), F32)
        for e in range(exp_dev):
            made = jnp.dot(hidden[e], wout[e, :, strip(dp_to[i])], preferred_element_type=F32)
            value = jnp.where(owner == e, made, value)
        part[i] = value
        if i:
            copies4[i] = to_dp(part.at[i], rpart.at[i], s4.at[i], r4.at[i], i)
            copies4[i].start()
    value = part[0]
    for i in range(1, n_dp):
        copies4[i].wait_recv()
        value = value + rpart[i]

    own5[...] = fold(value) if folded else value.astype(BF16).astype(F32)
    copies5 = launch(
        [to_ex(own5, recv5.at[i], s5.at[i], r5.at[i], i) for i in range(1, n_ex)]
    )
    copies6 = {}
    for b in range(n_ex):
        if b:
            copies5[b - 1].wait_recv()
        block_ref = recv5.at[b] if b else own5
        for i in dp_far:
            copies6[i, b] = to_dp(block_ref, recv6.at[i, b], s6.at[i, b], r6.at[i, b], i)
            copies6[i, b].start()
    for copy in copies2:
        copy.wait_send()
    mixing = mix[...]
    for i in range(n_dp):
        for b in range(n_ex):
            if i:
                copies6[i, b].wait_recv()
            item = recv6[i, b] if i else (recv5[b] if b else own5[...])
            send2[ex_from[b]] = item
        table = send2[...].astype(F32)
        if folded:
            table = jnp.concatenate([table[:, :per_dev, :], table[:, per_dev:, :]], axis=2)
        table = table.reshape(slots, cols).astype(BF16)
        out_ref[:, strip(dp_from[i])] = jnp.dot(
            mixing, table, preferred_element_type=F32
        ).astype(BF16)
    for copy in (
        stat_copies + list(num_copies.values()) + stat2_copies + copies3
        + list(copies4.values()) + copies5 + list(copies6.values())
    ):
        copy.wait_send()


def local(n_dp, n_ex, tokens, slot_param, pattern, w_in, w_out):
    rows, width = tokens.shape
    slots = slot_param.shape[1]
    cols = width // n_dp
    per_dev = slots // n_ex
    lanes = -(-slots // 128) * 128
    pieces = 4
    item = ((2 * per_dev, cols // 2), BF16) if cols % 256 == 0 else ((per_dev, cols), F32)
    dma = pltpu.SemaphoreType.DMA
    vmem, in_hbm = pl.BlockSpec(memory_space=pltpu.VMEM), pl.BlockSpec(memory_space=pltpu.HBM)
    return pl.pallas_call(
        functools.partial(slots_kernel, n_dp, n_ex, pieces),
        out_shape=jax.ShapeDtypeStruct((rows, width), BF16),
        in_specs=[in_hbm] * 5,
        out_specs=vmem,
        scratch_shapes=[
            pltpu.VMEM((slots, width), BF16),
            pltpu.VMEM(pattern.shape[::-1], pattern.dtype),
            pltpu.VMEM((rows, width), BF16),
            pltpu.VMEM(w_in.shape, BF16),
            pltpu.VMEM(w_out.shape, BF16),
            pltpu.VMEM((slots, rows), F32),
            pltpu.VMEM((slots, rows), BF16),
            pltpu.VMEM((rows, slots), BF16),
            pltpu.VMEM((8, lanes), F32),
            pltpu.VMEM((n_dp, 8, lanes), F32),
            pltpu.VMEM((n_dp, slots, cols), BF16),
            pltpu.VMEM((n_dp, slots, cols), BF16),
            pltpu.VMEM((8, lanes), F32),
            pltpu.VMEM((n_ex, 8, lanes), F32),
            pltpu.VMEM((n_ex,) + item[0], item[1]),
            pltpu.VMEM((n_ex,) + item[0], item[1]),
            pltpu.VMEM(*item),
            pltpu.VMEM((n_dp,) + item[0], item[1]),
            pltpu.VMEM((n_dp, per_dev, cols), F32),
            pltpu.VMEM((n_dp, per_dev, cols), F32),
            pltpu.VMEM(*item),
            pltpu.VMEM((n_ex,) + item[0], item[1]),
            pltpu.VMEM((n_dp, n_ex) + item[0], item[1]),
            dma((pieces,)),
            dma((4,)),
        ]
        + [
            dma(shape)
            for shape in (
                (n_dp,), (n_dp,), (n_ex,), (n_ex,), (n_dp,), (n_dp,), (n_ex,), (n_dp, n_ex)
            )
            for _ in range(2)
        ],
        compiler_params=pltpu.CompilerParams(
            collective_id=0, has_side_effects=True, vmem_limit_bytes=48 * 1024 * 1024
        ),
        cost_estimate=pl.CostEstimate(
            flops=6 * rows * width * slots + 4 * per_dev * w_in.size // w_in.shape[0],
            bytes_accessed=2 * (tokens.size + w_in.size + w_out.size),
            transcendentals=2 * rows * slots,
        ),
    )(tokens, slot_param.T, pattern.T, w_in, w_out)


def solution(mesh):
    return jax.shard_map(
        functools.partial(local, mesh.shape["dp"], mesh.shape["expert"]),
        mesh=mesh,
        in_specs=(
            P(("dp", "expert"), None),
            P(),
            P(None, ("dp", "expert")),
            P("expert", None, "dp"),
            P("expert", "dp", None),
        ),
        out_specs=P(("dp", "expert"), None),
        check_vma=False,
    )
```

time: 41 us -> 39.6 us (0.966)
  matrix products: 4.31 us -> 0 us
  local copies, waits for them, and re-layouts: 0 us -> 3.65 us
  Pallas kernels: 36.6 us -> 35.8 us
    dot_general x1 -> x0, matrix products: 4.31 us -> none  [local(): lax.dot_general(mixing, slot_out, (((0,), (0,)), ((), ())), preferred_ele...]
    unnamed x0 -> x5, local copies, waits for them, and re-layouts: none -> 3.65 us
    pallas_call x1, Pallas kernels: 36.6 us -> 35.8 us  [local(): pl.pallas_call(functools.partial(slots_kernel, n_dp, n_ex, pieces), out_s...]
where the time goes in v2:
time: 39.6 us; the launch traced here: 39.5 us
  Pallas kernels  35.8 us (90%)
  local copies, waits for them, and re-layouts  3.65 us (9%)
    pallas_call x1, Pallas kernels, local(): pl.pallas_call(functools.partial(slots_kernel, n_dp, n_ex, pieces), out_s...  35.8 us
    unnamed x5, local copies, waits for them, and re-layouts  3.65 us

profile of v2, /device:TPU:0, one launch (start us, length us, event | category | flops | bytes accessed | tf_op | source)
XLA Modules:
  0.0 39.5 jit_solution(16638926575192516048)
XLA Ops:
  0.0 0.0 copy-start
  0.0 0.9 %copy-done = bf16[2048,64]{0,1:T(8,128)(2,1)S(1)} copy-done((bf16[2048,64]{0,1:T(8,128)(2,1)S(1)}, bf16[2048,64]{0,1:T(8,128)(2,1)}, u32[]{:S(2)}) %copy-start) | copy-done | bytes 262168
  1.0 0.0 copy-start.1
  1.0 0.7 %copy-done.1 = s32[64,8]{0,1:T(8,128)S(1)} copy-done((s32[64,8]{0,1:T(8,128)S(1)}, s32[64,8]{0,1:T(8,128)}, u32[]{:S(2)}) %copy-start.1) | copy-done | bytes 2072
  1.6 35.8 %shard_map.55 = bf16[1024,2048]{1,0:T(8,128)(2,1)S(1)} custom-call(bf16[1024,2048]{1,0:T(8,128)(2,1)} %tok_hbm.1, bf16[64,2048]{1,0:T(8,128)(2,1)S(1)} %bitcast.2, s32[8,64]{1,0:T(8,128)S(1)} %bitcast.3, bf16[2,2048,1024]{2,1,0:T(8,128)(2,1)} %win_hbm.1, bf16[2,1024,2048]{2,1,0:T(8,128)(2,1)} %wout_hbm.1), custom_call_target="tpu_custom_call" | custom-call | flops 872415232 | bytes 20971520 | tf_op jit(solution)/shard_map/pallas_call | solution.py:293
  37.4 2.0 %copy.7 = bf16[1024,2048]{1,0:T(8,128)(2,1)} copy(bf16[1024,2048]{1,0:T(8,128)(2,1)S(1)} %shard_map.55) | data formatting | bytes 8388608
Async XLA Ops:
  0.0 0.9 %copy-start = (bf16[2048,64]{0,1:T(8,128)(2,1)S(1)}, bf16[2048,64]{0,1:T(8,128)(2,1)}, u32[]{:S(2)}) copy-start(bf16[2048,64]{0,1:T(8,128)(2,1)} %param.6) | copy-start | bytes 786436
  1.0 0.7 %copy-start.1 = (s32[64,8]{0,1:T(8,128)S(1)}, s32[64,8]{0,1:T(8,128)}, u32[]{:S(2)}) copy-start(s32[64,8]{0,1:T(8,128)} %param.7) | copy-start | bytes 6148

commit v3 on v2

--- a/solution.py
+++ b/solution.py
@@ -49,7 +49,7 @@
     slot_ref, pat_ref, tok, win, wout, logits, wts, mix,
     stat1, rstat1, num1, rnum1, stat2, rstat2,
     send2, recv2, xs, rx, part, rpart, own5, recv5, recv6,
-    tok_sem, w_sem,
+    tok_sem, w_sem, a_sem,
     ss1, rs1, sn1, rn1, ss2, rs2, s2, r2, s3, r3, s4, r4, s5, r5, s6, r6,
 ):
     d, k = lax.axis_index("dp"), lax.axis_index("expert")
@@ -93,8 +93,8 @@
         )
         for c in range(pieces)
     ]
-    load_slot = pltpu.make_async_copy(slot_hbm, slot_ref, w_sem.at[2])
-    load_pat = pltpu.make_async_copy(pat_hbm, pat_ref, w_sem.at[3])
+    load_slot = pltpu.make_async_copy(slot_hbm, slot_ref, a_sem.at[0])
+    load_pat = pltpu.make_async_copy(pat_hbm, pat_ref, a_sem.at[1])
     for load in [load_slot, load_pat] + loads:
         load.start()
     barrier = pltpu.get_barrier_semaphore()
@@ -106,8 +106,19 @@
         pl.semaphore_signal(
             barrier, inc=1, device_id={"expert": ex_to[i]}, device_id_type=MESH
         )
-    load_in = pltpu.make_async_copy(win_hbm, win, w_sem.at[0])
-    load_out = pltpu.make_async_copy(wout_hbm, wout, w_sem.at[1])
+
+    def in_parts(src, dst, first):
+        depth = src.shape[1] // 2
+        return [
+            pltpu.make_async_copy(
+                src.at[e, pl.ds(h * depth, depth)], dst.at[e, pl.ds(h * depth, depth)],
+                w_sem.at[first + 2 * e + h],
+            )
+            for e in range(exp_dev) for h in range(2)
+        ]
+
+    load_in = in_parts(win_hbm, win, 0)
+    load_out = in_parts(wout_hbm, wout, 2 * exp_dev)
 
     row_id = lax.broadcasted_iota(jnp.int32, (slots, lanes), 0)
     lane_id = lax.broadcasted_iota(jnp.int32, (slots, lanes), 1)
@@ -125,9 +136,9 @@
     for c in range(pieces):
         loads[c].wait()
         if c == pieces - 1:
-            load_in.start()
-            load_out.start()
-        logits[:, c * piece:(c + 1) * piece] = nt_dot(slot_t, tok[c * piece:(c + 1) * piece, :])
+            launch(load_in + load_out)
+        span = slice(c * piece, (c + 1) * piece)
+        logits[:, span] = nt_dot(tok[span, :], slot_t).T
 
     seen = pat_ref[...].astype(F32)
     if lanes > slots:
@@ -214,7 +225,8 @@
     xs[...] = value.astype(BF16).astype(xs.dtype)
 
     copies3 = launch([to_dp(xs, rx.at[i], s3.at[i], r3.at[i], i) for i in range(1, n_dp)])
-    load_in.wait()
+    for load in load_in:
+        load.wait()
     sums = [jnp.zeros((per_dev, hid), F32) for _ in range(exp_dev)]
     for i in range(n_dp):
         if i:
@@ -227,7 +239,8 @@
                 x, win[e, pl.ds(start, cols), :], preferred_element_type=F32
             )
     hidden = [gelu(s).astype(BF16) for s in sums]
-    load_out.wait()
+    for load in load_out:
+        load.wait()
     own_slots = per_dev // exp_dev
     owner = lax.broadcasted_iota(jnp.int32, (per_dev, cols), 0) // own_slots
     copies4 = {}
@@ -290,6 +303,8 @@
     item = ((2 * per_dev, cols // 2), BF16) if cols % 256 == 0 else ((per_dev, cols), F32)
     dma = pltpu.SemaphoreType.DMA
     vmem, in_hbm = pl.BlockSpec(memory_space=pltpu.VMEM), pl.BlockSpec(memory_space=pltpu.HBM)
+    operands = (tokens, slot_param.T, pattern.T, w_in, w_out)
+    placed = [pltpu.with_memory_space_constraint(x, pltpu.HBM) for x in operands]
     return pl.pallas_call(
         functools.partial(slots_kernel, n_dp, n_ex, pieces),
         out_shape=jax.ShapeDtypeStruct((rows, width), BF16),
@@ -320,7 +335,8 @@
             pltpu.VMEM((n_ex,) + item[0], item[1]),
             pltpu.VMEM((n_dp, n_ex) + item[0], item[1]),
             dma((pieces,)),
-            dma((4,)),
+            dma((4 * w_in.shape[0],)),
+            dma((2,)),
         ]
         + [
             dma(shape)
@@ -337,7 +353,7 @@
             bytes_accessed=2 * (tokens.size + w_in.size + w_out.size),
             transcendentals=2 * rows * slots,
         ),
-    )(tokens, slot_param.T, pattern.T, w_in, w_out)
+    )(*placed)
 
 
 def solution(mesh):

time: 39.6 us -> 38.7 us (0.977)
  local copies, waits for them, and re-layouts: 3.65 us -> 2.02 us
  Pallas kernels: 35.8 us -> 36.5 us
    unnamed x5 -> x1, local copies, waits for them, and re-layouts: 3.65 us -> 2.02 us
    pallas_call x1, Pallas kernels: 35.8 us -> 36.5 us  [local(): pl.pallas_call(functools.partial(slots_kernel, n_dp, n_ex, pieces), out_s...]
where the time goes in v3:
time: 38.7 us; the launch traced here: 38.5 us
  Pallas kernels  36.5 us (94%)
  local copies, waits for them, and re-layouts  2.02 us (5%)
    pallas_call x1, Pallas kernels, local(): pl.pallas_call(functools.partial(slots_kernel, n_dp, n_ex, pieces), out_s...  36.5 us
    unnamed x1, local copies, waits for them, and re-layouts  2.02 us

profile of v3, /device:TPU:0, one launch (start us, length us, event | category | flops | bytes accessed | tf_op | source)
XLA Modules:
  0.0 38.5 jit_solution(8041721065123351573)
XLA Ops:
  0.0 36.5 %shard_map.55 = bf16[1024,2048]{1,0:T(8,128)(2,1)S(1)} custom-call(bf16[1024,2048]{1,0:T(8,128)(2,1)} %tok_hbm.1, bf16[64,2048]{1,0:T(8,128)(2,1)} %bitcast.2, s32[8,64]{1,0:T(8,128)} %bitcast.3, bf16[2,2048,1024]{2,1,0:T(8,128)(2,1)} %win_hbm.1, bf16[2,1024,2048]{2,1,0:T(8,128)(2,1)} %wout_hbm.1), custom_call_target="tpu_custom_call" | custom-call | flops 872415232 | bytes 20971520 | tf_op jit(solution)/shard_map/pallas_call | solution.py:308
  36.5 2.0 %copy.7 = bf16[1024,2048]{1,0:T(8,128)(2,1)} copy(bf16[1024,2048]{1,0:T(8,128)(2,1)S(1)} %shard_map.55) | data formatting | bytes 8388608

commit v4 on v3

v4 whole, which is shorter than its diff:
```python
import functools

import jax
import jax.numpy as jnp
from jax import lax
from jax.experimental import pallas as pl
from jax.experimental.pallas import tpu as pltpu
from jax.sharding import PartitionSpec as P

MESH = pl.DeviceIdType.MESH
floor_value = -1e30
F32, BF16 = jnp.float32, jnp.bfloat16


def nt_dot(a, b):
    return lax.dot_general(a, b, (((1,), (1,)), ((), ())), preferred_element_type=F32)


def gelu(x):
    return 0.5 * x * (1.0 + jnp.tanh(0.7978845608028654 * (x + 0.044715 * (x * x * x))))


def fold(x):
    half = x.shape[-1] // 2
    return jnp.concatenate([x[..., :half], x[..., half:]], axis=x.ndim - 2)


def unfold(x):
    rows = x.shape[-2] // 2
    return jnp.concatenate([x[..., :rows, :], x[..., rows:, :]], axis=x.ndim - 1)


def flip(me, i, n):
    if n & (n - 1):
        return lax.rem(me + i, n), lax.rem(me + n - i, n)
    other, bit = 0, 1
    while bit < n:
        own = lax.rem(me // bit, 2)
        other = other + bit * ((1 - own) if i & bit else own)
        bit *= 2
    return other, other


def slots_kernel(
    n_dp, n_ex, pieces, strips,
    tok_hbm, slot_hbm, pat_hbm, win_hbm, wout_hbm,
    out_ref,
    slot_ref, pat_ref, tok, win, wout, logits, wts, mix, stat1, rstat1, stat2, rstat2, stat3, rstat3,
    num1, rnum1, send2, recv2, send3, recv3, part, rpart, own5, recv5, recv6, tab,
    tok_sem, w_sem, a_sem,
    ss1, rs1, ss2, rs2, ss3, rs3, s1, r1, s2, r2, s3, r3, s4, r4, s5, r5, s6, r6,
):
    d, k = lax.axis_index("dp"), lax.axis_index("expert")
    n_z = n_ex // 2
    z, c = k // 2, lax.rem(k, 2)
    slots, width = slot_ref.shape
    rows = tok.shape[0]
    cols = width // strips
    per_dev = slots // n_ex
    exp_dev, _, hid = win.shape
    blocks = pat_ref.shape[0]
    block = rows // blocks
    lanes = stat1.shape[1]
    piece = rows // pieces
    dp_to, _ = zip(*[flip(d, i, n_dp) for i in range(n_dp)])
    z_to, z_from = zip(*[flip(z, i, n_z) for i in range(n_z)])
    dp_far = list(range(n_dp - 1, 0, -1))
    z_far = list(range(n_z - 1, 0, -1))
    other = {"expert": 2 * z + 1 - c}
    dp_ids = [{"dp": target} for target in dp_to]
    z_ids = [{"expert": 2 * target + c} for target in z_to]

    def to(target, src, dst, ssem, rsem):
        return pltpu.make_async_remote_copy(
            src_ref=src, dst_ref=dst, send_sem=ssem, recv_sem=rsem,
            device_id=target, device_id_type=MESH,
        )

    sent = []

    def launch(copies):
        for copy in copies:
            copy.start()
        return copies

    def send(copies):
        sent.extend(copies)
        return launch(copies)

    def arrive(copies):
        for copy in copies:
            copy.wait_recv()

    loads = [
        pltpu.make_async_copy(
            tok_hbm.at[pl.ds(p * piece, piece)], tok.at[pl.ds(p * piece, piece)], tok_sem.at[p]
        )
        for p in range(pieces)
    ]
    load_slot = pltpu.make_async_copy(slot_hbm, slot_ref, a_sem.at[0])
    load_pat = pltpu.make_async_copy(pat_hbm, pat_ref, a_sem.at[1])
    launch([load_slot, load_pat] + loads)
    barrier = pltpu.get_barrier_semaphore()
    for target in [other] + dp_ids[1:] + z_ids[1:]:
        pl.semaphore_signal(barrier, inc=1, device_id=target, device_id_type=MESH)

    def in_parts(src, dst, first):
        depth = src.shape[1] // 2
        return [
            pltpu.make_async_copy(
                src.at[e, pl.ds(h * depth, depth)], dst.at[e, pl.ds(h * depth, depth)],
                w_sem.at[first + 2 * e + h],
            )
            for e in range(exp_dev) for h in range(2)
        ]

    load_in = in_parts(win_hbm, win, 0)
    load_out = in_parts(wout_hbm, wout, 2 * exp_dev)

    row_id = lax.broadcasted_iota(jnp.int32, (slots, lanes), 0)
    lane_id = lax.broadcasted_iota(jnp.int32, (slots, lanes), 1)
    eye = row_id == lane_id

    def as_column(row):
        return jnp.sum(jnp.where(eye, row, 0.0), axis=1, keepdims=True)

    own_shape = (2 * per_dev, lanes)
    own_row = lax.rem(lax.broadcasted_iota(jnp.int32, own_shape, 0), per_dev) + k * per_dev
    own_eye = own_row == lax.broadcasted_iota(jnp.int32, own_shape, 1)

    def own_column(row):
        return jnp.sum(jnp.where(own_eye, row, 0.0), axis=1, keepdims=True)

    def of_core(x):
        x = x.reshape(n_z, 2, per_dev, x.shape[-1])
        return jnp.where(c == 0, x[:, 0], x[:, 1]).reshape(n_z * per_dev, x.shape[-1])

    def as_row(column):
        return jnp.sum(jnp.where(eye, column, 0.0), axis=0, keepdims=True)

    load_slot.wait()
    load_pat.wait()
    slot_t = slot_ref[...]
    for p in range(pieces):
        loads[p].wait()
        if p == pieces - 1:
            launch(load_in + load_out)
        span = slice(p * piece, (p + 1) * piece)
        logits[:, span] = nt_dot(tok[span, :], slot_t).T

    seen = pat_ref[...].astype(F32)
    if lanes > slots:
        seen = jnp.concatenate([seen, jnp.zeros((blocks, lanes - slots), F32)], axis=1)
    columns = [as_column(seen[b:b + 1, :]) > 0.0 for b in range(blocks)]
    masked = [
        jnp.where(columns[b], logits[:, b * block:(b + 1) * block], floor_value)
        for b in range(blocks)
    ]
    top = masked[0]
    for b in range(1, blocks):
        top = jnp.maximum(top, masked[b])
    peak = jnp.max(top, axis=1, keepdims=True)
    total = jnp.zeros((slots, block), F32)
    for b in range(blocks):
        shifted = jnp.where(columns[b], masked[b] - peak, floor_value)
        weight = jnp.exp(shifted).astype(BF16)
        wts[:, b * block:(b + 1) * block] = weight
        total = total + weight.astype(F32)
    den = jnp.sum(total, axis=1, keepdims=True)
    stat_row = lax.broadcasted_iota(jnp.int32, stat1.shape, 0)
    stat1[...] = jnp.where(stat_row == 0, as_row(peak), as_row(den))

    def join(stats):
        high = stats[0][0:1]
        for stat in stats[1:]:
            high = jnp.maximum(high, stat[0:1])
        scales = [jnp.exp(stat[0:1] - high) for stat in stats]
        low = stats[0][1:2] * scales[0]
        for stat, scale in zip(stats[1:], scales[1:]):
            low = low + stat[1:2] * scale
        return high, low, scales

    pl.semaphore_wait(barrier, n_dp - 1 + n_z)
    stat_copy = send([to(other, stat1, rstat1, ss1, rs1)])
    weights = wts[...]
    copies1, copies2, copies3 = {}, {}, {}

    def numerator(j):
        made = jnp.dot(weights, tok[:, j * cols:(j + 1) * cols], preferred_element_type=F32)
        made = made.astype(BF16).astype(F32).reshape(n_z, 2, per_dev, cols)
        for side in range(2):
            num1[j, side] = made[:, side].reshape(n_z * per_dev, cols).astype(BF16)
        copies1[j] = send([to(other, num1.at[j, 1 - c], rnum1.at[j], s1.at[j], r1.at[j])])

    def over_core(j):
        arrive(copies1[j])
        joint = mine * num1[j, c].astype(F32) + theirs * rnum1[j].astype(F32)
        send2[j] = fold(joint.reshape(n_z, per_dev, cols)).astype(BF16)
        copies2[j] = send([
            to(z_ids[i], send2.at[j, z_to[i]], recv2.at[j, i], s2.at[j, i], r2.at[j, i])
            for i in z_far
        ])

    def over_z(j):
        arrive(copies2[j])
        value = z_scales[0] * send2[j, z].astype(F32)
        for i in range(1, n_z):
            value = value + z_scales[i] * recv2[j, i].astype(F32)
        send3[j] = value.astype(BF16)
        copies3[j] = send([
            to(dp_ids[i], send3.at[j], recv3.at[j, i], s3.at[j, i], r3.at[j, i]) for i in dp_far
        ])

    numerator(0)
    numerator(1)
    arrive(stat_copy)
    high, low, scales = join([stat1[...], rstat1[...]])
    stat2[...] = jnp.where(stat_row == 0, high, low)
    stat2_copies = send([
        to(z_ids[i], stat2, rstat2.at[i], ss2.at[i], rs2.at[i]) for i in z_far
    ])
    mine, theirs = [of_core(as_column(scale)) for scale in scales]
    over_core(0)
    for j in range(2, strips):
        numerator(j)
        over_core(j - 1)
    over_core(strips - 1)

    raw = logits[...]
    risen = jnp.exp(raw - jnp.max(raw, axis=0, keepdims=True))
    mix[...] = (risen / jnp.sum(risen, axis=0, keepdims=True)).T.astype(BF16)

    arrive(stat2_copies)
    high, low, scales = join([stat2[...]] + [rstat2[i] for i in range(1, n_z)])
    stat3[...] = jnp.where(stat_row == 0, high, low)
    stat3_copies = send([
        to(dp_ids[i], stat3, rstat3.at[i], ss3.at[i], rs3.at[i]) for i in dp_far
    ])
    z_scales = [own_column(scale) for scale in scales]
    for j in range(strips):
        over_z(j)
    arrive(stat3_copies)
    high, low, scales = join([stat3[...]] + [rstat3[i] for i in range(1, n_dp)])
    dp_scales = [own_column(scale / low) for scale in scales]
    for load in load_in:
        load.wait()
    sums = [jnp.zeros((per_dev, hid), F32) for _ in range(exp_dev)]
    for j in range(strips):
        arrive(copies3[j])
        value = dp_scales[0] * send3[j].astype(F32)
        for i in range(1, n_dp):
            value = value + dp_scales[i] * recv3[j, i].astype(F32)
        x = unfold(value).astype(BF16)
        for e in range(exp_dev):
            sums[e] = sums[e] + jnp.dot(
                x, win[e, j * cols:(j + 1) * cols, :], preferred_element_type=F32
            )

    hidden = [gelu(total).astype(BF16) for total in sums]
    for load in load_out:
        load.wait()
    own_slots = per_dev // exp_dev
    owner = lax.broadcasted_iota(jnp.int32, (per_dev, cols), 0) // own_slots
    copies4, copies5, copies6 = {}, {}, {}
    for j in range(strips):
        value = jnp.zeros((per_dev, cols), F32)
        for e in range(exp_dev):
            made = jnp.dot(
                hidden[e], wout[e, :, j * cols:(j + 1) * cols], preferred_element_type=F32
            )
            value = jnp.where(owner == e, made, value)
        part[j] = fold(value).astype(BF16)
        copies4[j] = send([
            to(dp_ids[i], part.at[j], rpart.at[j, i], s4.at[j, i], r4.at[j, i]) for i in dp_far
        ])

    def to_core(src, j, i):
        copies6[j, i] = send([to(other, src, recv6.at[j, i], s6.at[j, i], r6.at[j, i])])

    for j in range(strips):
        arrive(copies4[j])
        value = part[j].astype(F32)
        for i in range(1, n_dp):
            value = value + rpart[j, i].astype(F32)
        own5[j] = value.astype(BF16)
        copies5[j] = {
            i: send([to(z_ids[i], own5.at[j], recv5.at[j, i], s5.at[j, i], r5.at[j, i])])
            for i in z_far
        }
        to_core(own5.at[j], j, 0)
    mixing = mix[...]

    def pass_on(j):
        for i in range(1, n_z):
            arrive(copies5[j][i])
            to_core(recv5.at[j, i], j, i)

    def mixed(j):
        for i in range(n_z):
            arrive(copies6[j, i])
            tab[z_from[i], c] = recv5[j, i] if i else own5[j]
            tab[z_from[i], 1 - c] = recv6[j, i]
        table = unfold(tab[...].astype(F32).reshape(n_ex, 2 * per_dev, cols // 2))
        table = table.reshape(slots, cols).astype(BF16)
        out_ref[:, j * cols:(j + 1) * cols] = jnp.dot(
            mixing, table, preferred_element_type=F32
        ).astype(BF16)

    pass_on(0)
    for j in range(1, strips):
        pass_on(j)
        mixed(j - 1)
    mixed(strips - 1)
    for copy in sent:
        copy.wait_send()


def local(n_dp, n_ex, tokens, slot_param, pattern, w_in, w_out):
    rows, width = tokens.shape
    slots = slot_param.shape[1]
    per_dev = slots // n_ex
    lanes = -(-slots // 128) * 128
    n_z = n_ex // 2
    pieces, strips = 4, 4
    cols = width // strips
    flat = (2 * per_dev, cols // 2)
    dma = pltpu.SemaphoreType.DMA
    in_hbm = pl.BlockSpec(memory_space=pltpu.HBM)
    operands = (tokens, slot_param.T, pattern.T, w_in, w_out)
    placed = [pltpu.with_memory_space_constraint(x, pltpu.HBM) for x in operands]
    scratch = [
        ((slots, width), BF16),
        (pattern.shape[::-1], pattern.dtype),
        ((rows, width), BF16),
        (w_in.shape, BF16),
        (w_out.shape, BF16),
        ((slots, rows), F32),
        ((slots, rows), BF16),
        ((rows, slots), BF16),
        ((8, lanes), F32),
        ((8, lanes), F32),
        ((8, lanes), F32),
        ((n_z, 8, lanes), F32),
        ((8, lanes), F32),
        ((n_dp, 8, lanes), F32),
        ((strips, 2, n_z * per_dev, cols), BF16),
        ((strips, n_z * per_dev, cols), BF16),
        ((strips, n_z) + flat, BF16),
        ((strips, n_z) + flat, BF16),
        ((strips,) + flat, BF16),
        ((strips, n_dp) + flat, BF16),
        ((strips,) + flat, BF16),
        ((strips, n_dp) + flat, BF16),
        ((strips,) + flat, BF16),
        ((strips, n_z) + flat, BF16),
        ((strips, n_z) + flat, BF16),
        ((n_z, 2) + flat, BF16),
    ]
    by_z, by_dp = (strips, n_z), (strips, n_dp)
    remote = [None, (n_z,), (n_dp,), (strips,), by_z, by_dp, by_dp, by_z, by_z]
    return pl.pallas_call(
        functools.partial(slots_kernel, n_dp, n_ex, pieces, strips),
        out_shape=jax.ShapeDtypeStruct((rows, width), BF16),
        in_specs=[in_hbm] * 5,
        out_specs=pl.BlockSpec(memory_space=pltpu.VMEM),
        scratch_shapes=[pltpu.VMEM(*one) for one in scratch]
        + [dma((pieces,)), dma((4 * w_in.shape[0],)), dma((2,))]
        + [dma(shape) if shape else dma for shape in remote for _ in range(2)],
        compiler_params=pltpu.CompilerParams(
            collective_id=0, has_side_effects=True, vmem_limit_bytes=48 * 1024 * 1024
        ),
        cost_estimate=pl.CostEstimate(
            flops=6 * rows * width * slots + 4 * per_dev * w_in.size // w_in.shape[0],
            bytes_accessed=2 * (tokens.size + w_in.size + w_out.size),
            transcendentals=2 * rows * slots,
        ),
    )(*placed)


def solution(mesh):
    return jax.shard_map(
        functools.partial(local, mesh.shape["dp"], mesh.shape["expert"]),
        mesh=mesh,
        in_specs=(
            P(("dp", "expert"), None),
            P(),
            P(None, ("dp", "expert")),
            P("expert", None, "dp"),
            P("expert", "dp", None),
        ),
        out_specs=P(("dp", "expert"), None),
        check_vma=False,
    )
```

time: 38.7 us -> 31.6 us (0.82)
  Pallas kernels: 36.5 us -> 29.4 us
    pallas_call x1, Pallas kernels: 36.5 us -> 29.4 us  [local(): pl.pallas_call(functools.partial(slots_kernel, n_dp, n_ex, pieces, strips...]
where the time goes in v4:
time: 31.6 us; the launch traced here: 31.5 us
  Pallas kernels  29.4 us (93%)
  local copies, waits for them, and re-layouts  2.02 us (6%)
    pallas_call x1, Pallas kernels, local(): pl.pallas_call(functools.partial(slots_kernel, n_dp, n_ex, pieces, strips...  29.4 us
    unnamed x1, local copies, waits for them, and re-layouts  2.02 us

profile of v4, /device:TPU:0, one launch (start us, length us, event | category | flops | bytes accessed | tf_op | source)
XLA Modules:
  0.0 31.5 jit_solution(15470621789364974577)
XLA Ops:
  0.0 29.4 %shard_map.55 = bf16[1024,2048]{1,0:T(8,128)(2,1)S(1)} custom-call(bf16[1024,2048]{1,0:T(8,128)(2,1)} %tok_hbm.1, bf16[64,2048]{1,0:T(8,128)(2,1)} %bitcast.2, s32[8,64]{1,0:T(8,128)} %bitcast.3, bf16[2,2048,1024]{2,1,0:T(8,128)(2,1)} %win_hbm.1, bf16[2,1024,2048]{2,1,0:T(8,128)(2,1)} %wout_hbm.1), custom_call_target="tpu_custom_call" | custom-call | flops 872415232 | bytes 20971520 | tf_op jit(solution)/shard_map/pallas_call | solution.py:361
  29.5 2.0 %copy.7 = bf16[1024,2048]{1,0:T(8,128)(2,1)} copy(bf16[1024,2048]{1,0:T(8,128)(2,1)S(1)} %shard_map.55) | data formatting | bytes 8388608

commit v5 on v4

--- a/solution.py
+++ b/solution.py
@@ -10,10 +10,6 @@
 MESH = pl.DeviceIdType.MESH
 floor_value = -1e30
 F32, BF16 = jnp.float32, jnp.bfloat16
-
-
-def nt_dot(a, b):
-    return lax.dot_general(a, b, (((1,), (1,)), ((), ())), preferred_element_type=F32)
 
 
 def gelu(x):
@@ -45,7 +41,7 @@
     n_dp, n_ex, pieces, strips,
     tok_hbm, slot_hbm, pat_hbm, win_hbm, wout_hbm,
     out_ref,
-    slot_ref, pat_ref, tok, win, wout, logits, wts, mix, stat1, rstat1, stat2, rstat2, stat3, rstat3,
+    slot_ref, slot_in, mask, pat_ref, tok, win, wout, logits, wts, mix, stat1, rstat1, stat2, rstat2, stat3, rstat3,
     num1, rnum1, send2, recv2, send3, recv3, part, rpart, own5, recv5, recv6, tab,
     tok_sem, w_sem, a_sem,
     ss1, rs1, ss2, rs2, ss3, rs3, s1, r1, s2, r2, s3, r3, s4, r4, s5, r5, s6, r6,
@@ -140,33 +136,30 @@
 
     load_slot.wait()
     load_pat.wait()
-    slot_t = slot_ref[...]
+    slot_in[...] = slot_ref[...].astype(F32).T.astype(BF16)
+    seen = pat_ref[...].astype(F32)
+    if lanes > slots:
+        seen = jnp.concatenate([seen, jnp.zeros((blocks, lanes - slots), F32)], axis=1)
+    for b in range(blocks):
+        mask[:, b * block:(b + 1) * block] = jnp.broadcast_to(
+            as_column(seen[b:b + 1, :]), (slots, block)
+        )
+
+    top = jnp.full((slots, piece), floor_value, F32)
     for p in range(pieces):
         loads[p].wait()
         if p == pieces - 1:
             launch(load_in + load_out)
         span = slice(p * piece, (p + 1) * piece)
-        logits[:, span] = nt_dot(tok[span, :], slot_t).T
-
-    seen = pat_ref[...].astype(F32)
-    if lanes > slots:
-        seen = jnp.concatenate([seen, jnp.zeros((blocks, lanes - slots), F32)], axis=1)
-    columns = [as_column(seen[b:b + 1, :]) > 0.0 for b in range(blocks)]
-    masked = [
-        jnp.where(columns[b], logits[:, b * block:(b + 1) * block], floor_value)
-        for b in range(blocks)
-    ]
-    top = masked[0]
-    for b in range(1, blocks):
-        top = jnp.maximum(top, masked[b])
+        made = jnp.dot(tok[span, :], slot_in[...], preferred_element_type=F32).T
+        logits[:, span] = made
+        top = jnp.maximum(top, jnp.where(mask[:, span] > 0.0, made, floor_value))
     peak = jnp.max(top, axis=1, keepdims=True)
-    total = jnp.zeros((slots, block), F32)
-    for b in range(blocks):
-        shifted = jnp.where(columns[b], masked[b] - peak, floor_value)
-        weight = jnp.exp(shifted).astype(BF16)
-        wts[:, b * block:(b + 1) * block] = weight
-        total = total + weight.astype(F32)
-    den = jnp.sum(total, axis=1, keepdims=True)
+    raw = logits[...]
+    shifted = jnp.where(mask[...] > 0.0, raw - peak, floor_value)
+    weights = jnp.exp(shifted).astype(BF16)
+    wts[...] = weights
+    den = jnp.sum(weights.astype(F32), axis=1, keepdims=True)
     stat_row = lax.broadcasted_iota(jnp.int32, stat1.shape, 0)
     stat1[...] = jnp.where(stat_row == 0, as_row(peak), as_row(den))
 
@@ -330,6 +323,8 @@
     placed = [pltpu.with_memory_space_constraint(x, pltpu.HBM) for x in operands]
     scratch = [
         ((slots, width), BF16),
+        ((width, slots), BF16),
+        ((slots, rows), F32),
         (pattern.shape[::-1], pattern.dtype),
         ((rows, width), BF16),
         (w_in.shape, BF16),

time: 31.6 us -> 30.9 us (0.978)
  Pallas kernels: 29.4 us -> 28.8 us
    pallas_call x1, Pallas kernels: 29.4 us -> 28.8 us  [local(): pl.pallas_call(functools.partial(slots_kernel, n_dp, n_ex, pieces, strips...]
where the time goes in v5:
time: 30.9 us; the launch traced here: 30.8 us
  Pallas kernels  28.8 us (93%)
  local copies, waits for them, and re-layouts  2.02 us (7%)
    pallas_call x1, Pallas kernels, local(): pl.pallas_call(functools.partial(slots_kernel, n_dp, n_ex, pieces, strips...  28.8 us
    unnamed x1, local copies, waits for them, and re-layouts  2.02 us

profile of v5, /device:TPU:0, one launch (start us, length us, event | category | flops | bytes accessed | tf_op | source)
XLA Modules:
  0.0 30.8 jit_solution(5409679012052399948)
XLA Ops:
  0.0 28.8 %shard_map.55 = bf16[1024,2048]{1,0:T(8,128)(2,1)S(1)} custom-call(bf16[1024,2048]{1,0:T(8,128)(2,1)} %tok_hbm.1, bf16[64,2048]{1,0:T(8,128)(2,1)} %bitcast.2, s32[8,64]{1,0:T(8,128)} %bitcast.3, bf16[2,2048,1024]{2,1,0:T(8,128)(2,1)} %win_hbm.1, bf16[2,1024,2048]{2,1,0:T(8,128)(2,1)} %wout_hbm.1), custom_call_target="tpu_custom_call" | custom-call | flops 872415232 | bytes 20971520 | tf_op jit(solution)/shard_map/pallas_call | solution.py:356
  28.8 2.0 %copy.7 = bf16[1024,2048]{1,0:T(8,128)(2,1)} copy(bf16[1024,2048]{1,0:T(8,128)(2,1)S(1)} %shard_map.55) | data formatting | bytes 8388608

commit v6 on v5

--- a/solution.py
+++ b/solution.py
@@ -87,6 +87,13 @@
         for copy in copies:
             copy.wait_recv()
 
+    def arrive_all(landed, sem):
+        pltpu.make_async_copy(landed, landed, sem).wait()
+
+    def drain():
+        while sent:
+            sent.pop(0).wait_send()
+
     loads = [
         pltpu.make_async_copy(
             tok_hbm.at[pl.ds(p * piece, piece)], tok.at[pl.ds(p * piece, piece)], tok_sem.at[p]
@@ -174,9 +181,9 @@
         return high, low, scales
 
     pl.semaphore_wait(barrier, n_dp - 1 + n_z)
-    stat_copy = send([to(other, stat1, rstat1, ss1, rs1)])
+    stat_copy = send([to(other, stat1, rstat1, ss1.at[0], rs1.at[0])])
     weights = wts[...]
-    copies1, copies2, copies3 = {}, {}, {}
+    copies1 = {}
 
     def numerator(j):
         made = jnp.dot(weights, tok[:, j * cols:(j + 1) * cols], preferred_element_type=F32)
@@ -189,19 +196,19 @@
         arrive(copies1[j])
         joint = mine * num1[j, c].astype(F32) + theirs * rnum1[j].astype(F32)
         send2[j] = fold(joint.reshape(n_z, per_dev, cols)).astype(BF16)
-        copies2[j] = send([
-            to(z_ids[i], send2.at[j, z_to[i]], recv2.at[j, i], s2.at[j, i], r2.at[j, i])
+        send([
+            to(z_ids[i], send2.at[j, z_to[i]], recv2.at[j, i], s2.at[j, i], r2.at[j])
             for i in z_far
         ])
 
     def over_z(j):
-        arrive(copies2[j])
+        arrive_all(recv2.at[j, pl.ds(1, n_z - 1)], r2.at[j])
         value = z_scales[0] * send2[j, z].astype(F32)
         for i in range(1, n_z):
             value = value + z_scales[i] * recv2[j, i].astype(F32)
         send3[j] = value.astype(BF16)
-        copies3[j] = send([
-            to(dp_ids[i], send3.at[j], recv3.at[j, i], s3.at[j, i], r3.at[j, i]) for i in dp_far
+        send([
+            to(dp_ids[i], send3.at[j], recv3.at[j, i], s3.at[j, i], r3.at[j]) for i in dp_far
         ])
 
     numerator(0)
@@ -209,8 +216,8 @@
     arrive(stat_copy)
     high, low, scales = join([stat1[...], rstat1[...]])
     stat2[...] = jnp.where(stat_row == 0, high, low)
-    stat2_copies = send([
-        to(z_ids[i], stat2, rstat2.at[i], ss2.at[i], rs2.at[i]) for i in z_far
+    send([
+        to(z_ids[i], stat2, rstat2.at[i], ss2.at[i], rs2) for i in z_far
     ])
     mine, theirs = [of_core(as_column(scale)) for scale in scales]
     over_core(0)
@@ -223,23 +230,23 @@
     risen = jnp.exp(raw - jnp.max(raw, axis=0, keepdims=True))
     mix[...] = (risen / jnp.sum(risen, axis=0, keepdims=True)).T.astype(BF16)
 
-    arrive(stat2_copies)
+    arrive_all(rstat2.at[pl.ds(1, n_z - 1)], rs2)
     high, low, scales = join([stat2[...]] + [rstat2[i] for i in range(1, n_z)])
     stat3[...] = jnp.where(stat_row == 0, high, low)
-    stat3_copies = send([
-        to(dp_ids[i], stat3, rstat3.at[i], ss3.at[i], rs3.at[i]) for i in dp_far
+    send([
+        to(dp_ids[i], stat3, rstat3.at[i], ss3.at[i], rs3) for i in dp_far
     ])
     z_scales = [own_column(scale) for scale in scales]
     for j in range(strips):
         over_z(j)
-    arrive(stat3_copies)
+    arrive_all(rstat3.at[pl.ds(1, n_dp - 1)], rs3)
     high, low, scales = join([stat3[...]] + [rstat3[i] for i in range(1, n_dp)])
     dp_scales = [own_column(scale / low) for scale in scales]
     for load in load_in:
         load.wait()
     sums = [jnp.zeros((per_dev, hid), F32) for _ in range(exp_dev)]
     for j in range(strips):
-        arrive(copies3[j])
+        arrive_all(recv3.at[j, pl.ds(1, n_dp - 1)], r3.at[j])
         value = dp_scales[0] * send3[j].astype(F32)
         for i in range(1, n_dp):
             value = value + dp_scales[i] * recv3[j, i].astype(F32)
@@ -254,7 +261,9 @@
         load.wait()
     own_slots = per_dev // exp_dev
     owner = lax.broadcasted_iota(jnp.int32, (per_dev, cols), 0) // own_slots
-    copies4, copies5, copies6 = {}, {}, {}
+    copies5 = {}
+    early = list(sent)
+    sent.clear()
     for j in range(strips):
         value = jnp.zeros((per_dev, cols), F32)
         for e in range(exp_dev):
@@ -263,15 +272,17 @@
             )
             value = jnp.where(owner == e, made, value)
         part[j] = fold(value).astype(BF16)
-        copies4[j] = send([
-            to(dp_ids[i], part.at[j], rpart.at[j, i], s4.at[j, i], r4.at[j, i]) for i in dp_far
+        send([
+            to(dp_ids[i], part.at[j], rpart.at[j, i], s4.at[j, i], r4.at[j]) for i in dp_far
         ])
 
     def to_core(src, j, i):
-        copies6[j, i] = send([to(other, src, recv6.at[j, i], s6.at[j, i], r6.at[j, i])])
-
+        send([to(other, src, recv6.at[j, i], s6.at[j, i], r6.at[j])])
+
+    for copy in early:
+        copy.wait_send()
     for j in range(strips):
-        arrive(copies4[j])
+        arrive_all(rpart.at[j, pl.ds(1, n_dp - 1)], r4.at[j])
         value = part[j].astype(F32)
         for i in range(1, n_dp):
             value = value + rpart[j, i].astype(F32)
@@ -282,6 +293,10 @@
         }
         to_core(own5.at[j], j, 0)
     mixing = mix[...]
+    late = sent[:(n_dp - 1) * strips]
+    del sent[:(n_dp - 1) * strips]
+    for copy in late:
+        copy.wait_send()
 
     def pass_on(j):
         for i in range(1, n_z):
@@ -289,8 +304,8 @@
             to_core(recv5.at[j, i], j, i)
 
     def mixed(j):
+        arrive_all(recv6.at[j], r6.at[j])
         for i in range(n_z):
-            arrive(copies6[j, i])
             tab[z_from[i], c] = recv5[j, i] if i else own5[j]
             tab[z_from[i], 1 - c] = recv6[j, i]
         table = unfold(tab[...].astype(F32).reshape(n_ex, 2 * per_dev, cols // 2))
@@ -303,9 +318,8 @@
     for j in range(1, strips):
         pass_on(j)
         mixed(j - 1)
+    drain()
     mixed(strips - 1)
-    for copy in sent:
-        copy.wait_send()
 
 
 def local(n_dp, n_ex, tokens, slot_param, pattern, w_in, w_out):
@@ -352,7 +366,8 @@
         ((n_z, 2) + flat, BF16),
     ]
     by_z, by_dp = (strips, n_z), (strips, n_dp)
-    remote = [None, (n_z,), (n_dp,), (strips,), by_z, by_dp, by_dp, by_z, by_z]
+    leave = [(1,), (n_z,), (n_dp,), (strips,), by_z, by_dp, by_dp, by_z, by_z]
+    come = [(1,), None, None, (strips,), (strips,), (strips,), (strips,), by_z, (strips,)]
     return pl.pallas_call(
         functools.partial(slots_kernel, n_dp, n_ex, pieces, strips),
         out_shape=jax.ShapeDtypeStruct((rows, width), BF16),
@@ -360,7 +375,7 @@
         out_specs=pl.BlockSpec(memory_space=pltpu.VMEM),
         scratch_shapes=[pltpu.VMEM(*one) for one in scratch]
         + [dma((pieces,)), dma((4 * w_in.shape[0],)), dma((2,))]
-        + [dma(shape) if shape else dma for shape in remote for _ in range(2)],
+        + [dma(shape) if shape else dma for pair in zip(leave, come) for shape in pair],
         compiler_params=pltpu.CompilerParams(
             collective_id=0, has_side_effects=True, vmem_limit_bytes=48 * 1024 * 1024
         ),

time: 30.9 us -> 30.4 us (0.984)
  Pallas kernels: 28.8 us -> 28.2 us
    pallas_call x1, Pallas kernels: 28.8 us -> 28.2 us  [local(): pl.pallas_call(functools.partial(slots_kernel, n_dp, n_ex, pieces, strips...]
where the time goes in v6:
time: 30.4 us; the launch traced here: 30.2 us
  Pallas kernels  28.2 us (93%)
  local copies, waits for them, and re-layouts  2.02 us (7%)
    pallas_call x1, Pallas kernels, local(): pl.pallas_call(functools.partial(slots_kernel, n_dp, n_ex, pieces, strips...  28.2 us
    unnamed x1, local copies, waits for them, and re-layouts  2.02 us

profile of v6, /device:TPU:0, one launch (start us, length us, event | category | flops | bytes accessed | tf_op | source)
XLA Modules:
  0.0 30.2 jit_solution(15681605177427616101)
XLA Ops:
  0.0 28.2 %shard_map.55 = bf16[1024,2048]{1,0:T(8,128)(2,1)S(1)} custom-call(bf16[1024,2048]{1,0:T(8,128)(2,1)} %tok_hbm.1, bf16[64,2048]{1,0:T(8,128)(2,1)} %bitcast.2, s32[8,64]{1,0:T(8,128)} %bitcast.3, bf16[2,2048,1024]{2,1,0:T(8,128)(2,1)} %win_hbm.1, bf16[2,1024,2048]{2,1,0:T(8,128)(2,1)} %wout_hbm.1), custom_call_target="tpu_custom_call" | custom-call | flops 872415232 | bytes 20971520 | tf_op jit(solution)/shard_map/pallas_call | solution.py:371
  28.2 2.0 %copy.7 = bf16[1024,2048]{1,0:T(8,128)(2,1)} copy(bf16[1024,2048]{1,0:T(8,128)(2,1)S(1)} %shard_map.55) | data formatting | bytes 8388608

commit v7 on v6

--- a/solution.py
+++ b/solution.py
@@ -328,7 +328,7 @@
     per_dev = slots // n_ex
     lanes = -(-slots // 128) * 128
     n_z = n_ex // 2
-    pieces, strips = 4, 4
+    pieces, strips = 4, 8
     cols = width // strips
     flat = (2 * per_dev, cols // 2)
     dma = pltpu.SemaphoreType.DMA

time: 30.4 us -> 35.4 us (1.16)
  Pallas kernels: 28.2 us -> 33.2 us
    pallas_call x1, Pallas kernels: 28.2 us -> 33.2 us  [local(): pl.pallas_call(functools.partial(slots_kernel, n_dp, n_ex, pieces, strips...]
where the time goes in v7:
time: 35.4 us; the launch traced here: 35.3 us
  Pallas kernels  33.2 us (94%)
  local copies, waits for them, and re-layouts  2.02 us (6%)
    pallas_call x1, Pallas kernels, local(): pl.pallas_call(functools.partial(slots_kernel, n_dp, n_ex, pieces, strips...  33.2 us
    unnamed x1, local copies, waits for them, and re-layouts  2.02 us

profile of v7, /device:TPU:0, one launch (start us, length us, event | category | flops | bytes accessed | tf_op | source)
XLA Modules:
  0.0 35.3 jit_solution(2899194223483946161)
XLA Ops:
  0.0 33.2 %shard_map.55 = bf16[1024,2048]{1,0:T(8,128)(2,1)S(1)} custom-call(bf16[1024,2048]{1,0:T(8,128)(2,1)} %tok_hbm.1, bf16[64,2048]{1,0:T(8,128)(2,1)} %bitcast.2, s32[8,64]{1,0:T(8,128)} %bitcast.3, bf16[2,2048,1024]{2,1,0:T(8,128)(2,1)} %win_hbm.1, bf16[2,1024,2048]{2,1,0:T(8,128)(2,1)} %wout_hbm.1), custom_call_target="tpu_custom_call" | custom-call | flops 872415232 | bytes 20971520 | tf_op jit(solution)/shard_map/pallas_call | solution.py:371
  33.2 2.0 %copy.7 = bf16[1024,2048]{1,0:T(8,128)(2,1)} copy(bf16[1024,2048]{1,0:T(8,128)(2,1)S(1)} %shard_map.55) | data formatting | bytes 8388608

commit v8 on v6

--- a/solution.py
+++ b/solution.py
@@ -42,7 +42,7 @@
     tok_hbm, slot_hbm, pat_hbm, win_hbm, wout_hbm,
     out_ref,
     slot_ref, slot_in, mask, pat_ref, tok, win, wout, logits, wts, mix, stat1, rstat1, stat2, rstat2, stat3, rstat3,
-    num1, rnum1, send2, recv2, send3, recv3, part, rpart, own5, recv5, recv6, tab,
+    num1, rnum1, send2, recv2, send3, recv3, part, rpart, recv5, recv6, tab,
     tok_sem, w_sem, a_sem,
     ss1, rs1, ss2, rs2, ss3, rs3, s1, r1, s2, r2, s3, r3, s4, r4, s5, r5, s6, r6,
 ):
@@ -276,9 +276,6 @@
             to(dp_ids[i], part.at[j], rpart.at[j, i], s4.at[j, i], r4.at[j]) for i in dp_far
         ])
 
-    def to_core(src, j, i):
-        send([to(other, src, recv6.at[j, i], s6.at[j, i], r6.at[j])])
-
     for copy in early:
         copy.wait_send()
     for j in range(strips):
@@ -286,12 +283,11 @@
         value = part[j].astype(F32)
         for i in range(1, n_dp):
             value = value + rpart[j, i].astype(F32)
-        own5[j] = value.astype(BF16)
+        recv5[j, 0] = value.astype(BF16)
         copies5[j] = {
-            i: send([to(z_ids[i], own5.at[j], recv5.at[j, i], s5.at[j, i], r5.at[j, i])])
+            i: send([to(z_ids[i], recv5.at[j, 0], recv5.at[j, i], s5.at[j, i], r5.at[j, i])])
             for i in z_far
         }
-        to_core(own5.at[j], j, 0)
     mixing = mix[...]
     late = sent[:(n_dp - 1) * strips]
     del sent[:(n_dp - 1) * strips]
@@ -301,12 +297,12 @@
     def pass_on(j):
         for i in range(1, n_z):
             arrive(copies5[j][i])
-            to_core(recv5.at[j, i], j, i)
+        send([to(other, recv5.at[j], recv6.at[j], s6.at[j], r6.at[j])])
 
     def mixed(j):
         arrive_all(recv6.at[j], r6.at[j])
         for i in range(n_z):
-            tab[z_from[i], c] = recv5[j, i] if i else own5[j]
+            tab[z_from[i], c] = recv5[j, i]
             tab[z_from[i], 1 - c] = recv6[j, i]
         table = unfold(tab[...].astype(F32).reshape(n_ex, 2 * per_dev, cols // 2))
         table = table.reshape(slots, cols).astype(BF16)
@@ -360,13 +356,12 @@
         ((strips, n_dp) + flat, BF16),
         ((strips,) + flat, BF16),
         ((strips, n_dp) + flat, BF16),
-        ((strips,) + flat, BF16),
         ((strips, n_z) + flat, BF16),
         ((strips, n_z) + flat, BF16),
         ((n_z, 2) + flat, BF16),
     ]
     by_z, by_dp = (strips, n_z), (strips, n_dp)
-    leave = [(1,), (n_z,), (n_dp,), (strips,), by_z, by_dp, by_dp, by_z, by_z]
+    leave = [(1,), (n_z,), (n_dp,), (strips,), by_z, by_dp, by_dp, by_z, (strips,)]
     come = [(1,), None, None, (strips,), (strips,), (strips,), (strips,), by_z, (strips,)]
     return pl.pallas_call(
         functools.partial(slots_kernel, n_dp, n_ex, pieces, strips),

time: 30.4 us -> 30.3 us (level)
  no operation moved by 1% of the time
where the time goes in v8:
time: 30.3 us; the launch traced here: 30.1 us
  Pallas kernels  28.1 us (93%)
  local copies, waits for them, and re-layouts  2.02 us (7%)
    pallas_call x1, Pallas kernels, local(): pl.pallas_call(functools.partial(slots_kernel, n_dp, n_ex, pieces, strips...  28.1 us
    unnamed x1, local copies, waits for them, and re-layouts  2.02 us

profile of v8, /device:TPU:0, one launch (start us, length us, event | category | flops | bytes accessed | tf_op | source)
XLA Modules:
  0.0 30.1 jit_solution(677453710911270705)
XLA Ops:
  0.0 28.1 %shard_map.55 = bf16[1024,2048]{1,0:T(8,128)(2,1)S(1)} custom-call(bf16[1024,2048]{1,0:T(8,128)(2,1)} %tok_hbm.1, bf16[64,2048]{1,0:T(8,128)(2,1)} %bitcast.2, s32[8,64]{1,0:T(8,128)} %bitcast.3, bf16[2,2048,1024]{2,1,0:T(8,128)(2,1)} %win_hbm.1, bf16[2,1024,2048]{2,1,0:T(8,128)(2,1)} %wout_hbm.1), custom_call_target="tpu_custom_call" | custom-call | flops 872415232 | bytes 20971520 | tf_op jit(solution)/shard_map/pallas_call | solution.py:366
  28.1 2.0 %copy.7 = bf16[1024,2048]{1,0:T(8,128)(2,1)} copy(bf16[1024,2048]{1,0:T(8,128)(2,1)S(1)} %shard_map.55) | data formatting | bytes 8388608
